TPU v7x, 512 devices: a whole 4x4x16 slice. The times are simulated.
512 devices in a mesh: pair: 64 (over x, z), virt: 8 (over y, core).
Axes of the slice: x: 4, y: 4, z: 16, core: 2. Of those that a mesh axis runs over, the one named last changes fastest.
Arguments:
- amplitudes: float32 [128, 512, 512], P('pair', 'virt'), may hold values from -6 to 6
- integral_store: float32 [8, 64, 128, 128], P('virt', 'pair'), may hold values from -0.1875 to 0.1875
- domains: int32 [128, 4], P('pair'), may hold values from 0 to 7, as said below
- domain_length: int32 [128], P('pair'), may hold values from 1 to 4
- owner_map: int32 [64], replicated, may hold values from 0 to 63, each once
Outputs:
- ladder: float32 [128, 512, 512], P('pair', 'virt')
Inputs may be any that keep to these rules, and one draw needn't show every extreme that they name: `domains`: each row names 4 different tiles; only the first domain_length entries of a row are live.
All inputs are finite; a program needn't handle non-finite values.
Results may differ from a plain program's by a relative error of at most 0.000098.
Values sent between devices are 32-bit elements; how exact they have to be, the bound alone decides.
No kernel may reach another device: no remote copies, remote signals or barrier semaphores. Data moves between devices by JAX's collectives and lax.ppermute only.
A program may use at most 64 MiB of HBM per device.

v0:
```python
import jax
import jax.numpy as jnp
from jax import lax
from jax.sharding import PartitionSpec as P

TILE = 128
M = 4
NT = 8


def ladder_term(matrix, masked):
    half = jnp.einsum("qrc,cd->qrd", matrix, masked, precision=lax.Precision.HIGHEST)
    return jnp.einsum("qrd,qbd->rb", half, matrix, precision=lax.Precision.HIGHEST)


def on_device(amplitudes, integral_store, domains, domain_length, owner_map):
    order = M * TILE
    full_amps = lax.all_gather(amplitudes, "virt", axis=1, tiled=True)
    whole_store = lax.all_gather(integral_store, "pair", axis=1, tiled=True)
    local_q = integral_store.shape[0]
    pairs = amplitudes.shape[0]
    live = (jnp.arange(M)[None, :] < domain_length[:, None]).astype(jnp.float32)
    position = owner_map[domains[:, :, None] * NT + domains[:, None, :]]
    picked = jnp.take(whole_store, position.reshape(-1), axis=1)
    picked = picked.reshape(local_q, pairs, M, M, TILE, TILE)
    picked = picked * (live[:, :, None] * live[:, None, :])[None, :, :, :, None, None]
    matrices = picked.transpose(1, 0, 2, 4, 3, 5).reshape(pairs, local_q, order, order)
    row_live = jnp.repeat(live, TILE, axis=1)
    masked = full_amps * row_live[:, :, None] * row_live[:, None, :]

    def one_pair(items):
        matrix, amp_block, length = items
        return ladder_term(matrix, amp_block)

    terms = lax.map(one_pair, (matrices, masked, domain_length))
    summed = lax.psum(terms, "virt")
    rows = order // lax.axis_size("virt")
    return lax.dynamic_slice_in_dim(summed, lax.axis_index("virt") * rows, rows, 1)


def solution(mesh):
    placed = (
        P("pair", "virt", None),
        P("virt", "pair", None, None),
        P("pair", None),
        P("pair"),
        P(),
    )
    return jax.shard_map(
        on_device, mesh=mesh, in_specs=placed, out_specs=P("pair", "virt", None), check_vma=False
    )
```

profile of v0, /device:TPU:2, one launch (start us, length us, event | category | flops | bytes accessed | tf_op | source)
XLA Modules:
  0.0 300.7 jit_solution(1592998112843832967)
XLA Ops:
  6.5 0.7 all-gather.5.cloned.1.call-update
  7.3 0.7 all-gather.3.cloned.1.call-update
  8.1 0.7 broadcast_multiply_fusion.1
  8.7 0.8 compare_select_fusion.1
  9.5 0.1 reshape.131
  9.6 0.7 gather_fusion
  10.3 0.1 reshape.130
  10.4 0.1 compare_convert_fusion
  10.5 0.1 broadcast_bitcast_fusion
  10.6 0.1 broadcast_multiply_fusion
  10.7 36.2 %all-gather.5.cloned.1.call-done = f32[2,512,512]{2,1,0:T(8,128)} async-done(((f32[2,64,512]{2,1,0:T(8,128)}), f32[2,512,512]{2,1,0:T(8,128)}) %all-gather.5.cloned.1.call-update) | async-done | bytes 2097168 | tf_op jit(solution)/shard_map/all_gather | solution.py:18
  46.8 3.2 %multiply_multiply_fusion = f32[2,512,512]{2,1,0:T(8,128)} fusion(f32[2,512,512]{2,1,0:T(8,128)} %all-gather.5.cloned.1.call-done, f32[2,512]{1,0:T(2,128)S(1)} %bitcast.44), kind=kLoop, calls=%fused_computation.13 | loop fusion | flops 1048576 | bytes 4198400 | tf_op jit(solution)/shard_map/mul | solution.py:29
  50.0 145.4 %all-gather.3.cloned.1.call-done = f32[1,64,128,128]{3,2,0,1:T(8,128)} async-done(((f32[1,1,128,128]{3,2,0,1:T(8,128)}), f32[1,64,128,128]{3,2,0,1:T(8,128)}) %all-gather.3.cloned.1.call-update) | async-done | bytes 4194320 | tf_op jit(solution)/shard_map/all_gather | solution.py:19
  195.4 2.9 gather_fusion.1
  198.3 0.3 multiply_bitcast_fusion
  198.6 2.7 copy.9
  201.3 2.1 reshape.128
  203.4 11.9 %while.10 = (s32[]{:T(128)}, f32[2,512,512]{2,1,0:T(8,128)}, f32[2,1,512,512]{3,2,1,0:T(8,128)S(1)}, f32[2,512,512]{2,1,0:T(8,128)}, s32[]{:T(128)}) while((s32[]{:T(128)}, f32[2,512,512]{2,1,0:T(8,128)}, f32[2,1,512,512]{3,2,1,0:T(8,128)S(1)}, f32[2,512,512]{2,1,0:T(8,128)}, s32[]{:T(128)}) %tuple.18), condition=%wide.region_1.2_spmd, body=%wide.region_0.1_spmd.sunk | while | flops 3221225472 | bytes 6293565 | solution.py:35
  203.4 3.1 %fusion.22 = f32[512,512]{1,0:T(8,128)S(1)} fusion(f32[2,512,512]{2,1,0:T(8,128)} %get-tuple-element.74, s32[]{:T(128)} %get-tuple-element.66, f32[2,1,512,512]{3,2,1,0:T(8,128)S(1)} %get-tuple-element.73), kind=kOutput, calls=%fused_computation.4.clone.1 | convolution fusion | flops 1610612736 | bytes 3146752 | tf_op jit(solution)/shard_map/while/body/eval_jaxpr/qrc,cd->qrd/dot_general | solution.py:12
  206.5 2.9 fusion.23
  209.3 3.1 %fusion.22 = f32[512,512]{1,0:T(8,128)S(1)} fusion(f32[2,512,512]{2,1,0:T(8,128)} %get-tuple-element.74, s32[]{:T(128)} %get-tuple-element.66, f32[2,1,512,512]{3,2,1,0:T(8,128)S(1)} %get-tuple-element.73), kind=kOutput, calls=%fused_computation.4.clone.1 | convolution fusion | flops 1610612736 | bytes 3146752 | tf_op jit(solution)/shard_map/while/body/eval_jaxpr/qrc,cd->qrd/dot_general | solution.py:12
  212.4 2.9 fusion.23
  215.3 77.2 %all-reduce.2.cloned.1.call-done = f32[2,512,512]{2,1,0:T(8,128)} async-done(((f32[2,512,512]{2,1,0:T(8,128)}), f32[2,512,512]{2,1,0:T(8,128)}) %all-reduce.2.cloned.1.call-update) | async-done | bytes 2097168 | tf_op jit(solution)/shard_map/psum | solution.py:36
  292.5 1.7 constant_dynamic-slice_fusion
  (14 shorter events, 0.1 us)
Async XLA Ops:
  6.5 3.1 %copy-start = (s32[64]{0:T(128)S(1)}, s32[64]{0:T(128)}, u32[]{:S(2)}) copy-start(s32[64]{0:T(128)} %param.11) | copy-start | bytes 772
  6.5 40.3 %all-gather.5.cloned.1.call-start = ((), (), s32[]{:S(2)}) async-start(), calls=%async_computation.1 | async-start | bytes 2359296 | tf_op jit(solution)/shard_map/all_gather | solution.py:18
  7.3 188.2 %all-gather.3.cloned.1.call-start = ((), (), s32[]{:S(2)}) async-start(), calls=%async_computation | async-start | bytes 4259840 | tf_op jit(solution)/shard_map/all_gather | solution.py:19
  8.0 284.5 %all-reduce.2.cloned.1.call-start = ((), (), s32[]{:S(2)}) async-start(), calls=%async_computation.2 | async-start | bytes 4194304 | tf_op jit(solution)/shard_map/psum | solution.py:36
  9.6 0.8 copy-start.1
Sparse Core Ops, SparseCore 0:
  9.5 37.3 all-gather.4
  49.8 145.5 all-gather.2
  215.4 77.0 all-reduce.1
where the time goes:
time: 301 us
  waiting for transfers between devices  260 us (86%)
  between operations  13.2 us (4%)
  matrix products  11.9 us (4%)
  local copies, waits for them, and re-layouts  10.3 us (3%)
  other arithmetic  5.04 us (2%)
    all_gather x1, waiting for transfers between devices, on_device(): whole_store = lax.all_gather(integral_store, 'pair', axis=1, tiled=True)  145 us
    psum x1, waiting for transfers between devices, on_device(): summed = lax.psum(terms, 'virt')  77.2 us
    all_gather x1, waiting for transfers between devices, on_device(): full_amps = lax.all_gather(amplitudes, 'virt', axis=1, tiled=True)  36.2 us
    dot_general x2, matrix products, ladder_term(): jnp.einsum('qrc,cd->qrd', matrix, masked, precision=lax.Precision.HIGHEST)  6.15 us
  transfers between devices with their start and end apart: 3, of which 3 were waited for; matrix products, arithmetic and copies ran while one was open for 2% of the time, Pallas kernels for 0%

commit v1 on v0

--- a/solution.py
+++ b/solution.py
@@ -2,10 +2,22 @@
 import jax.numpy as jnp
 from jax import lax
 from jax.sharding import PartitionSpec as P
+from jax.lax import axis_index, axis_size, ppermute
 
 TILE = 128
 M = 4
 NT = 8
+
+
+def series_spread(local_array, lane_axis):
+    count_all = axis_size(lane_axis)
+    vals = tuple(((ix, (ix + 1) % count_all) for ix in range(count_all)))
+    z_new = [None] * count_all
+    z_new[count_all - 1] = local_array
+    for dev in range(count_all - 2, -1, -1):
+        z_new[dev] = ppermute(z_new[dev + 1], lane_axis, vals)
+    block_now = jnp.concatenate(z_new, 1)
+    return jnp.roll(block_now, (axis_index(lane_axis) + 1) * local_array.shape[1], 1)
 
 
 def ladder_term(matrix, masked):
@@ -15,7 +27,7 @@
 
 def on_device(amplitudes, integral_store, domains, domain_length, owner_map):
     order = M * TILE
-    full_amps = lax.all_gather(amplitudes, "virt", axis=1, tiled=True)
+    full_amps = series_spread(amplitudes, lane_axis="virt")
     whole_store = lax.all_gather(integral_store, "pair", axis=1, tiled=True)
     local_q = integral_store.shape[0]
     pairs = amplitudes.shape[0]

time: 301 us -> 266 us (0.88)
  waiting for transfers between devices: 260 us -> 225 us
    ppermute x0 -> x7, waiting for transfers between devices: none -> 46 us  [series_spread(): z_new[dev] = ppermute(z_new[dev + 1], lane_axis, vals)]
    all_gather x1, waiting for transfers between devices: 145 us -> 101 us  [on_device(): whole_store = lax.all_gather(integral_store, 'pair', axis=1, tiled=True)]
    all_gather x1 -> x0, waiting for transfers between devices: 36.2 us -> none  [on_device(): full_amps = lax.all_gather(amplitudes, 'virt', axis=1, tiled=True)]
  transfers between devices with their start and end apart: 3 -> 9, of which waited for: 3 -> 9; matrix products, arithmetic and copies ran while one was open for 2% -> 2% of each run, Pallas kernels for 0% -> 0%
where the time goes in v1:
time: 266 us
  waiting for transfers between devices  225 us (85%)
  between operations  13.6 us (5%)
  matrix products  11.9 us (4%)
  local copies, waits for them, and re-layouts  10.6 us (4%)
  other arithmetic  4.11 us (2%)
    all_gather x1, waiting for transfers between devices, on_device(): whole_store = lax.all_gather(integral_store, 'pair', axis=1, tiled=True)  101 us
    psum x1, waiting for transfers between devices, on_device(): summed = lax.psum(terms, 'virt')  77.2 us
    ppermute x7, waiting for transfers between devices, series_spread(): z_new[dev] = ppermute(z_new[dev + 1], lane_axis, vals)  46 us
    dot_general x2, matrix products, ladder_term(): jnp.einsum('qrc,cd->qrd', matrix, masked, precision=lax.Precision.HIGHEST)  6.15 us
    dot_general x2, matrix products, ladder_term(): jnp.einsum('qrd,qbd->rb', half, matrix, precision=lax.Precision.HIGHEST)  5.75 us
  transfers between devices with their start and end apart: 9, of which 9 were waited for; matrix products, arithmetic and copies ran while one was open for 2% of the time, Pallas kernels for 0%

profile of v1, /device:TPU:2, one launch (start us, length us, event | category | flops | bytes accessed | tf_op | source)
XLA Modules:
  0.0 265.6 jit_solution(2595661007710129526)
XLA Ops:
  6.5 0.7 all-gather.2.cloned.1.call-update
  7.3 7.2 %collective-permute-done = f32[2,64,512]{2,1,0:T(8,128)S(1)} collective-permute-done((f32[2,64,512]{2,1,0:T(8,128)}, f32[2,64,512]{2,1,0:T(8,128)S(1)}, u32[]{:S(2)}, u32[]{:S(2)}) %collective-permute-start) | collective-permute-done | bytes 262176 | tf_op jit(solution)/shard_map/ppermute | solution.py:18
  14.5 7.0 %collective-permute-done.1 = f32[2,64,512]{2,1,0:T(8,128)S(1)} collective-permute-done((f32[2,64,512]{2,1,0:T(8,128)S(1)}, f32[2,64,512]{2,1,0:T(8,128)S(1)}, u32[]{:S(2)}, u32[]{:S(2)}) %collective-permute-start.1) | collective-permute-done | bytes 262176 | tf_op jit(solution)/shard_map/ppermute | solution.py:18
  21.5 0.7 broadcast_multiply_fusion.1
  22.2 6.3 %collective-permute-done.2 = f32[2,64,512]{2,1,0:T(8,128)S(1)} collective-permute-done((f32[2,64,512]{2,1,0:T(8,128)S(1)}, f32[2,64,512]{2,1,0:T(8,128)S(1)}, u32[]{:S(2)}, u32[]{:S(2)}) %collective-permute-start.2) | collective-permute-done | bytes 262176 | tf_op jit(solution)/shard_map/ppermute | solution.py:18
  28.6 0.8 compare_select_fusion.1
  29.4 0.7 compare_convert_fusion
  30.1 5.4 %collective-permute-done.3 = f32[2,64,512]{2,1,0:T(8,128)S(1)} collective-permute-done((f32[2,64,512]{2,1,0:T(8,128)S(1)}, f32[2,64,512]{2,1,0:T(8,128)S(1)}, u32[]{:S(2)}, u32[]{:S(2)}) %collective-permute-start.3) | collective-permute-done | bytes 262176 | tf_op jit(solution)/shard_map/ppermute | solution.py:18
  35.6 0.7 gather_fusion
  36.4 6.2 %collective-permute-done.4 = f32[2,64,512]{2,1,0:T(8,128)S(1)} collective-permute-done((f32[2,64,512]{2,1,0:T(8,128)S(1)}, f32[2,64,512]{2,1,0:T(8,128)S(1)}, u32[]{:S(2)}, u32[]{:S(2)}) %collective-permute-start.4) | collective-permute-done | bytes 262176 | tf_op jit(solution)/shard_map/ppermute | solution.py:18
  42.7 6.9 %collective-permute-done.5 = f32[2,64,512]{2,1,0:T(8,128)S(1)} collective-permute-done((f32[2,64,512]{2,1,0:T(8,128)S(1)}, f32[2,64,512]{2,1,0:T(8,128)S(1)}, u32[]{:S(2)}, u32[]{:S(2)}) %collective-permute-start.5) | collective-permute-done | bytes 262176 | tf_op jit(solution)/shard_map/ppermute | solution.py:18
  49.7 6.9 %collective-permute-done.6 = f32[2,64,512]{2,1,0:T(8,128)S(1)} collective-permute-done((f32[2,64,512]{2,1,0:T(8,128)S(1)}, f32[2,64,512]{2,1,0:T(8,128)S(1)}, u32[]{:S(2)}, u32[]{:S(2)}) %collective-permute-start.6) | collective-permute-done | bytes 262176 | tf_op jit(solution)/shard_map/ppermute | solution.py:18
  57.0 1.6 multiply_multiply_fusion
  58.6 101.4 %all-gather.2.cloned.1.call-done = f32[1,64,128,128]{3,2,0,1:T(8,128)} async-done(((f32[1,1,128,128]{3,2,0,1:T(8,128)}), f32[1,64,128,128]{3,2,0,1:T(8,128)}) %all-gather.2.cloned.1.call-update) | async-done | bytes 4194320 | tf_op jit(solution)/shard_map/all_gather | solution.py:31
  160.0 2.9 %gather_fusion.1 = f32[32,128,128]{2,1,0:T(8,128)S(1)} fusion(f32[64,128,128]{2,1,0:T(8,128)} %bitcast.42, s32[1024]{0:T(1024)S(1)} %pad_clamp_fusion), kind=kCustom, calls=%fused_computation.1 | custom fusion | bytes 4194432 | tf_op jit(solution)/shard_map/jit(_take)/gather | solution.py:36
  163.2 2.7 %copy.9 = f32[2,1,4,128,4,128]{5,4,3,2,0,1:T(4,128)} copy(f32[2,1,4,128,4,128]{5,3,4,2,0,1:T(8,128)S(1)} %multiply_bitcast_fusion) | data formatting | bytes 4194304 | tf_op jit(solution)/shard_map/transpose | solution.py:39
  165.8 2.1 reshape.128
  167.9 11.9 %while.10 = (s32[]{:T(128)}, f32[2,512,512]{2,1,0:T(8,128)}, f32[2,1,512,512]{3,2,1,0:T(8,128)S(1)}, f32[2,512,512]{2,1,0:T(8,128)}, s32[]{:T(128)}) while((s32[]{:T(128)}, f32[2,512,512]{2,1,0:T(8,128)}, f32[2,1,512,512]{3,2,1,0:T(8,128)S(1)}, f32[2,512,512]{2,1,0:T(8,128)}, s32[]{:T(128)}) %tuple.18), condition=%wide.region_1.2_spmd, body=%wide.region_0.1_spmd.sunk | while | flops 3221225472 | bytes 6293565 | solution.py:47
  167.9 3.1 %fusion.22 = f32[512,512]{1,0:T(8,128)S(1)} fusion(f32[2,512,512]{2,1,0:T(8,128)} %get-tuple-element.74, s32[]{:T(128)} %get-tuple-element.66, f32[2,1,512,512]{3,2,1,0:T(8,128)S(1)} %get-tuple-element.73), kind=kOutput, calls=%fused_computation.4.clone.1 | convolution fusion | flops 1610612736 | bytes 3146752 | tf_op jit(solution)/shard_map/while/body/eval_jaxpr/qrc,cd->qrd/dot_general | solution.py:24
  171.0 2.9 %fusion.23 = f32[2,512,512]{2,1,0:T(8,128)} fusion(f32[2,512,512]{2,1,0:T(8,128)} %get-tuple-element.67, s32[]{:T(128)} %get-tuple-element.66, f32[512,512]{1,0:T(8,128)S(1)} %fusion.22, f32[2,1,512,512]{3,2,1,0:T(8,128)S(1)} %get-tuple-element.73), kind=kOutput, calls=%fused_computation.3.clone.1 | convolution fusion | flops 1610612736 | bytes 3146752 | tf_op jit(solution)/shard_map/while/body/eval_jaxpr/qrd,qbd->rb/dot_general | solution.py:25
  173.9 3.1 %fusion.22 = f32[512,512]{1,0:T(8,128)S(1)} fusion(f32[2,512,512]{2,1,0:T(8,128)} %get-tuple-element.74, s32[]{:T(128)} %get-tuple-element.66, f32[2,1,512,512]{3,2,1,0:T(8,128)S(1)} %get-tuple-element.73), kind=kOutput, calls=%fused_computation.4.clone.1 | convolution fusion | flops 1610612736 | bytes 3146752 | tf_op jit(solution)/shard_map/while/body/eval_jaxpr/qrc,cd->qrd/dot_general | solution.py:24
  177.0 2.9 %fusion.23 = f32[2,512,512]{2,1,0:T(8,128)} fusion(f32[2,512,512]{2,1,0:T(8,128)} %get-tuple-element.67, s32[]{:T(128)} %get-tuple-element.66, f32[512,512]{1,0:T(8,128)S(1)} %fusion.22, f32[2,1,512,512]{3,2,1,0:T(8,128)S(1)} %get-tuple-element.73), kind=kOutput, calls=%fused_computation.3.clone.1 | convolution fusion | flops 1610612736 | bytes 3146752 | tf_op jit(solution)/shard_map/while/body/eval_jaxpr/qrd,qbd->rb/dot_general | solution.py:25
  179.9 77.2 %all-reduce.2.cloned.1.call-done = f32[2,512,512]{2,1,0:T(8,128)} async-done(((f32[2,512,512]{2,1,0:T(8,128)}), f32[2,512,512]{2,1,0:T(8,128)}) %all-reduce.2.cloned.1.call-update) | async-done | bytes 2097168 | tf_op jit(solution)/shard_map/psum | solution.py:48
  257.1 1.7 constant_dynamic-slice_fusion
  (41 shorter events, 1.0 us)
Async XLA Ops:
  6.5 29.0 %copy-start = (s32[64]{0:T(128)S(1)}, s32[64]{0:T(128)}, u32[]{:S(2)}) copy-start(s32[64]{0:T(128)} %param.11) | copy-start | bytes 772
  6.5 50.2 %copy-start.1 = (f32[2,64,512]{2,1,0:T(8,128)S(1)}, f32[2,64,512]{2,1,0:T(8,128)}, u32[]{:S(2)}) copy-start(f32[2,64,512]{2,1,0:T(8,128)} %param.7) | copy-start | bytes 786436
  6.5 153.5 %all-gather.2.cloned.1.call-start = ((), (), s32[]{:S(2)}) async-start(), calls=%async_computation | async-start | bytes 4259840 | tf_op jit(solution)/shard_map/all_gather | solution.py:31
  7.3 249.9 %all-reduce.2.cloned.1.call-start = ((), (), s32[]{:S(2)}) async-start(), calls=%async_computation.1 | async-start | bytes 4194304 | tf_op jit(solution)/shard_map/psum | solution.py:48
  7.3 7.2 %collective-permute-start = (f32[2,64,512]{2,1,0:T(8,128)}, f32[2,64,512]{2,1,0:T(8,128)S(1)}, u32[]{:S(2)}, u32[]{:S(2)}) collective-permute-start(f32[2,64,512]{2,1,0:T(8,128)} %param.7), channel_id=1, source_target_pairs={{0,1},{1,2},{2,3},{3,4},{4,5},{5,6},{6,7},{7,0},{8,9},{9,10},{10,1... | collective-permute-start | bytes 786440 | tf_op jit(solution)/shard_map/ppermute | solution.py:18
  14.5 7.0 %collective-permute-start.1 = (f32[2,64,512]{2,1,0:T(8,128)S(1)}, f32[2,64,512]{2,1,0:T(8,128)S(1)}, u32[]{:S(2)}, u32[]{:S(2)}) collective-permute-start(f32[2,64,512]{2,1,0:T(8,128)S(1)} %collective-permute-done), channel_id=1, source_target_pairs={{0,1},{1,2},{2,3},{3,4},{4,5},{5,6},{6,7},{7,0},{8,9},{9,10},{10,1... | collective-permute-start | bytes 786440 | tf_op jit(solution)/shard_map/ppermute | solution.py:18
  21.5 7.0 %collective-permute-start.2 = (f32[2,64,512]{2,1,0:T(8,128)S(1)}, f32[2,64,512]{2,1,0:T(8,128)S(1)}, u32[]{:S(2)}, u32[]{:S(2)}) collective-permute-start(f32[2,64,512]{2,1,0:T(8,128)S(1)} %collective-permute-done.1), channel_id=1, source_target_pairs={{0,1},{1,2},{2,3},{3,4},{4,5},{5,6},{6,7},{7,0},{8,9},{9,10},{10,1... | collective-permute-start | bytes 786440 | tf_op jit(solution)/shard_map/ppermute | solution.py:18
  28.6 7.0 %collective-permute-start.3 = (f32[2,64,512]{2,1,0:T(8,128)S(1)}, f32[2,64,512]{2,1,0:T(8,128)S(1)}, u32[]{:S(2)}, u32[]{:S(2)}) collective-permute-start(f32[2,64,512]{2,1,0:T(8,128)S(1)} %collective-permute-done.2), channel_id=1, source_target_pairs={{0,1},{1,2},{2,3},{3,4},{4,5},{5,6},{6,7},{7,0},{8,9},{9,10},{10,1... | collective-permute-start | bytes 786440 | tf_op jit(solution)/shard_map/ppermute | solution.py:18
  35.6 7.0 %collective-permute-start.4 = (f32[2,64,512]{2,1,0:T(8,128)S(1)}, f32[2,64,512]{2,1,0:T(8,128)S(1)}, u32[]{:S(2)}, u32[]{:S(2)}) collective-permute-start(f32[2,64,512]{2,1,0:T(8,128)S(1)} %collective-permute-done.3), channel_id=1, source_target_pairs={{0,1},{1,2},{2,3},{3,4},{4,5},{5,6},{6,7},{7,0},{8,9},{9,10},{10,1... | collective-permute-start | bytes 786440 | tf_op jit(solution)/shard_map/ppermute | solution.py:18
  42.6 7.0 %collective-permute-start.5 = (f32[2,64,512]{2,1,0:T(8,128)S(1)}, f32[2,64,512]{2,1,0:T(8,128)S(1)}, u32[]{:S(2)}, u32[]{:S(2)}) collective-permute-start(f32[2,64,512]{2,1,0:T(8,128)S(1)} %collective-permute-done.4), channel_id=1, source_target_pairs={{0,1},{1,2},{2,3},{3,4},{4,5},{5,6},{6,7},{7,0},{8,9},{9,10},{10,1... | collective-permute-start | bytes 786440 | tf_op jit(solution)/shard_map/ppermute | solution.py:18
  49.6 7.0 %collective-permute-start.6 = (f32[2,64,512]{2,1,0:T(8,128)S(1)}, f32[2,64,512]{2,1,0:T(8,128)S(1)}, u32[]{:S(2)}, u32[]{:S(2)}) collective-permute-start(f32[2,64,512]{2,1,0:T(8,128)S(1)} %collective-permute-done.5), channel_id=1, source_target_pairs={{0,1},{1,2},{2,3},{3,4},{4,5},{5,6},{6,7},{7,0},{8,9},{9,10},{10,1... | collective-permute-start | bytes 786440 | tf_op jit(solution)/shard_map/ppermute | solution.py:18
Sparse Core Ops, SparseCore 0:
  10.3 149.6 all-gather.1
  180.0 77.0 all-reduce.1
